TPU v7x, 32 devices: a whole 2x2x4 slice. The times are simulated.
32 devices in a mesh: group: 2 (over y), head: 4 (over z), row: 2 (over x), sub: 2 (over core).
Axes of the slice: x: 2, y: 2, z: 4, core: 2. Of those that a mesh axis runs over, the one named last changes fastest.
Arguments:
- query_latent: bfloat16 [256, 1536], P(('group', 'row')), parts along dimension 0, may hold values from -6 to 6
- kv_cache: bfloat16 [256, 128, 512], P(('group', 'row', 'head')), parts along dimension 0, may hold values from -70 to 70
- row_lengths: int32 [256], P(('group', 'row')), parts along dimension 0, may hold values from 1 to 128
- head_map: int32 [128], replicated, may hold values from 0 to 127, as said below
- uq_stored: bfloat16 [128, 1536, 128], P('sub', 'head', 'row'), may hold values from -0.15625 to 0.15625
- uk_stored: bfloat16 [128, 512, 128], P('sub', 'head', 'row'), may hold values from -0.25 to 0.25
- uv_stored: bfloat16 [128, 512, 128], P('sub', 'head', 'row'), may hold values from -0.25 to 0.25
- out_stored: bfloat16 [128, 128, 7168], P('sub', 'head', 'row'), may hold values from -0.5 to 0.5
Outputs:
- attn_output: bfloat16 [256, 7168], P(('group', 'head', 'sub'), 'row'), parts along dimension 0
There are 2 independent parts, one for each index of `group`. A program takes and returns all parts, laid end to end along the dimension named above; an argument that names none is the same for every part. Nothing has to cross between parts.
Inputs may be any that keep to these rules, and one draw needn't show every extreme that they name: `head_map`: slots s * 64 to (s + 1) * 64 - 1 hold every head of that same range once.
All inputs are finite; a program needn't handle non-finite values.
Results may differ from a plain program's by a relative error of at most 0.012.
Values may be sent and summed in bfloat16 or wider, within the bound.
A program may use at most 128 MiB of HBM per device.

v0:
```python
import math

import jax
import jax.numpy as jnp
from jax import lax
from jax.sharding import PartitionSpec as P

DH = 128


def form_pair(query_up, key_up, value_up, out_up):
    absorbed_q = jnp.einsum(
        "hqd,hkd->hqk", query_up, key_up, preferred_element_type=jnp.float32
    ).astype(jnp.bfloat16)
    absorbed_o = jnp.einsum(
        "hkd,hdo->hko", value_up, out_up, preferred_element_type=jnp.float32
    ).astype(jnp.bfloat16)
    return (absorbed_q, absorbed_o)


def attend(running, queries, lengths, block_rows, first_pos, score_scale):
    best, mass, accum = running
    width = block_rows.shape[1]
    scores = (
        jnp.einsum("rhk,rtk->rht", queries, block_rows, preferred_element_type=jnp.float32)
        * score_scale
    )
    positions = first_pos + jnp.arange(width, dtype=jnp.int32)
    alive = (positions[None, :] < lengths[:, None])[:, None, :]
    scores = jnp.where(alive, scores, -1e30)
    newest = jnp.maximum(best, jnp.max(scores, axis=2))
    weights = jnp.where(alive, jnp.exp(scores - newest[:, :, None]), 0.0)
    factor = jnp.exp(best - newest)
    mass = mass * factor + jnp.sum(weights, axis=2)
    accum = accum * factor[:, :, None] + jnp.einsum(
        "rht,rtk->rhk", weights, block_rows.astype(jnp.float32), precision=lax.Precision.HIGHEST
    )
    return (newest, mass, accum)


def local(
    query_latent, kv_cache, row_lengths, head_map, uq_stored, uk_stored, uv_stored, out_stored
):
    slots = uq_stored.shape[0]
    first_slot = lax.axis_index("sub") * slots
    local_map = lax.dynamic_slice_in_dim(head_map, first_slot, slots, 0)
    slot_order = jnp.argsort(local_map)
    query_up = jnp.take(uq_stored, slot_order, axis=0)
    key_up = jnp.take(uk_stored, slot_order, axis=0)
    value_up = jnp.take(uv_stored, slot_order, axis=0)
    query_up, key_up, value_up, out_up = (
        lax.all_to_all(query_up, "head", split_axis=0, concat_axis=1, tiled=True),
        lax.all_to_all(key_up, "head", split_axis=0, concat_axis=1, tiled=True),
        lax.all_to_all(value_up, "head", split_axis=0, concat_axis=1, tiled=True),
        lax.all_to_all(out_stored, "head", split_axis=0, concat_axis=1, tiled=True),
    )
    query_up, key_up, value_up = (
        lax.all_gather(query_up, "row", axis=2, tiled=True),
        lax.all_gather(key_up, "row", axis=2, tiled=True),
        lax.all_gather(value_up, "row", axis=2, tiled=True),
    )
    absorbed_q, absorbed_o = form_pair(query_up, key_up, value_up, out_up)
    query_lat = jnp.einsum(
        "rq,hqk->rhk", query_latent, absorbed_q, preferred_element_type=jnp.float32
    ).astype(jnp.bfloat16)
    score_scale = 1.0 / math.sqrt(DH)
    head_count = query_lat.shape[1]
    latent_width = query_lat.shape[2]
    piece = lax.all_gather(kv_cache, "head", axis=0, tiled=True)
    count = piece.shape[0]
    half = piece.shape[1] // 2
    state = (
        jnp.full((count, head_count), -1e30, jnp.float32),
        jnp.zeros((count, head_count), jnp.float32),
        jnp.zeros((count, head_count, latent_width), jnp.float32),
    )
    state = attend(state, query_lat, row_lengths, piece[:, :half], 0, score_scale)
    state = attend(state, query_lat, row_lengths, piece[:, half:], half, score_scale)
    best, mass, accum = state
    result = accum / mass[:, :, None]
    attended = result.astype(jnp.bfloat16)
    gathered = lax.all_gather(attended, "row", axis=0, tiled=True)
    summed = lax.psum_scatter(
        jnp.einsum("rhk,hko->ro", gathered, absorbed_o, preferred_element_type=jnp.float32),
        ("head", "sub"),
        scatter_dimension=0,
        tiled=True,
    )
    return summed.astype(jnp.bfloat16)


def solution(mesh):
    in_specs = (
        P(("group", "row"), None),
        P(("group", "row", "head"), None, None),
        P(("group", "row")),
        P(),
        P("sub", "head", "row"),
        P("sub", "head", "row"),
        P("sub", "head", "row"),
        P("sub", "head", "row"),
    )
    out_specs = P(("group", "head", "sub"), "row")
    return jax.shard_map(local, mesh=mesh, in_specs=in_specs, out_specs=out_specs, check_vma=False)
```

profile of v0, /device:TPU:13, one launch (start us, length us, event | category | flops | bytes accessed | tf_op | source)
XLA Modules:
  0.0 733.3 jit_solution(12497658808855078742)
XLA Ops:
  7.4 2.0 sort.17
  9.5 2.9 gather_fusion.1
  12.4 2.9 gather_fusion.2
  15.3 3.1 broadcast_select_fusion.2
  18.4 4.8 all-to-all-start.1
  23.2 2.6 gather_fusion
  25.8 3.9 broadcast_select_fusion
  29.7 15.3 %all-to-all-done.1 = bf16[64,128,64]{1,2,0:T(8,128)(2,1)} async-done(((bf16[64,128,64]{1,2,0:T(8,128)(2,1)}), bf16[64,128,64]{1,2,0:T(8,128)(2,1)}, u32[]{:S(2)}, u32[]{:S(2)}) %all-to-all-start.1) | async-done | bytes 1048608 | tf_op jit(solution)/shard_map/all_to_all | solution.py:53
  45.0 7.2 all-to-all-start
  52.2 3.1 copy.51
  55.3 2.3 all_to_all.59
  57.6 60.8 %all-to-all-done = bf16[64,384,64]{1,2,0:T(8,128)(2,1)S(1)} async-done(((bf16[64,384,64]{1,2,0:T(8,128)(2,1)}), bf16[64,384,64]{1,2,0:T(8,128)(2,1)S(1)}, u32[]{:S(2)}, u32[]{:S(2)}) %all-to-all-start) | async-done | bytes 3145760 | tf_op jit(solution)/shard_map/all_to_all | solution.py:52
  118.4 4.2 copy.49
  122.7 6.1 all_to_all.55
  128.8 1.2 copy-done.2
  130.0 29.5 %all_to_all.72 = bf16[64,128,64]{1,2,0:T(8,128)(2,1)S(1)} all-to-all(bf16[64,128,64]{1,2,0:T(8,128)(2,1)S(1)} %copy-done.2), channel_id=1, replica_groups=mesh['group'=2,'head'=4,'row'=2,'sub'=2] {'head'}, dimensions={0} | all-to-all | bytes 2097152 | tf_op jit(solution)/shard_map/all_to_all | solution.py:54
  159.5 8.4 %all-to-all-start.3 = ((bf16[64,32,3584]{2,1,0:T(8,128)(2,1)}), bf16[64,32,3584]{2,1,0:T(8,128)(2,1)}, u32[]{:S(2)}, u32[]{:S(2)}) async-start(bf16[64,32,3584]{2,1,0:T(8,128)(2,1)} %param.17), calls=%async_computation.3 | async-start | bytes 29360128 | tf_op jit(solution)/shard_map/all_to_all | solution.py:55
  168.8 0.9 copy.50
  169.7 1.3 all_to_all.63
  171.2 41.6 %all-gather.6.cloned.1.call-done = bf16[16,1536,128]{1,2,0:T(8,128)(2,1)} async-done(((bf16[16,1536,64]{1,2,0:T(8,128)(2,1)}), bf16[16,1536,128]{1,2,0:T(8,128)(2,1)}) %all-gather.6.cloned.1.call-update) | async-done | bytes 6291472 | tf_op jit(solution)/shard_map/all_gather | solution.py:58
  212.8 13.4 %fusion.25 = bf16[64,16,512]{2,0,1:T(8,128)(2,1)S(1)} fusion(bf16[16,1536,128]{1,2,0:T(8,128)(2,1)} %all-gather.6.cloned.1.call-done, bf16[16,512,128]{1,2,0:T(8,128)(2,1)} %all-gather.8.cloned.1.call-done, bf16[64,1536]{1,0:T(8,128)(2,1)S(1)} %copy-done.5), kind=kOutput, calls=%fused_computation.23 | convolution fusion | flops 4844945408 | bytes 9633792 | tf_op jit(solution)/shard_map/rq,hqk->rhk/dot_general | solution.py:63
  226.2 359.1 %all-gather.10.cloned.1.call-done = bf16[64,128,512]{2,1,0:T(8,128)(2,1)} async-done(((bf16[16,128,512]{2,1,0:T(8,128)(2,1)}), bf16[64,128,512]{2,1,0:T(8,128)(2,1)}) %all-gather.10.cloned.1.call-update) | async-done | bytes 8388624 | tf_op jit(solution)/shard_map/all_gather | solution.py:69
  585.4 3.7 fusion.54
  589.1 3.5 fusion.55
  593.3 1.8 fusion.11
  595.2 2.9 divide_convert_fusion
  598.3 17.4 %all-to-all-done.3 = bf16[64,32,3584]{2,1,0:T(8,128)(2,1)} async-done(((bf16[64,32,3584]{2,1,0:T(8,128)(2,1)}), bf16[64,32,3584]{2,1,0:T(8,128)(2,1)}, u32[]{:S(2)}, u32[]{:S(2)}) %all-to-all-start.3) | async-done | bytes 14680096 | tf_op jit(solution)/shard_map/all_to_all | solution.py:55
  615.7 13.6 %copy.34 = bf16[16,4,32,3584]{3,2,1,0:T(8,128)(2,1)} copy(bf16[16,4,32,3584]{3,2,0,1:T(8,128)(2,1)} %bitcast.9) | data formatting | bytes 29360128 | tf_op jit(solution)/shard_map/all_to_all | solution.py:55
  629.3 27.0 %all-gather.12.cloned.1.call-done = bf16[128,16,512]{2,1,0:T(8,128)(2,1)} async-done(((bf16[64,16,512]{2,1,0:T(8,128)(2,1)}), bf16[128,16,512]{2,1,0:T(8,128)(2,1)}) %all-gather.12.cloned.1.call-update) | async-done | bytes 2097168 | tf_op jit(solution)/shard_map/all_gather | solution.py:82
  656.3 39.2 %fusion.8 = f32[128,3584]{1,0:T(8,128)} fusion(bf16[16,512,128]{1,2,0:T(8,128)(2,1)} %all-gather.14.cloned.1.call-done, bf16[16,128,3584]{2,1,0:T(8,128)(2,1)} %bitcast.33, bf16[128,16,512]{2,1,0:T(8,128)(2,1)} %all-gather.12.cloned.1.call-done), kind=kOutput, calls=%fused_computation.9 | convolution fusion | flops 15061745664 | bytes 20709376 | tf_op jit(solution)/shard_map/rhk,hko->ro/dot_general | solution.py:84
  695.5 29.4 %reduce-scatter.2.cloned.1.call-done = f32[16,3584]{1,0:T(8,128)} async-done(((f32[128,3584]{1,0:T(8,128)}), f32[16,3584]{1,0:T(8,128)}) %reduce-scatter.2.cloned.1.call-update) | async-done | bytes 229392 | tf_op jit(solution)/shard_map/reduce_scatter | solution.py:83
  724.9 1.6 convert_element_type.25
  (35 shorter events, 3.1 us)
Async XLA Ops:
  6.5 16.6 %copy-start = (bf16[64,384,64]{1,2,0:T(8,128)(2,1)S(1)}, bf16[64,384,64]{1,2,0:T(8,128)(2,1)}, u32[]{:S(2)}) copy-start(bf16[64,384,64]{1,2,0:T(8,128)(2,1)} %param.14) | copy-start | bytes 9437188
  18.4 26.6 %all-to-all-start.1 = ((bf16[64,128,64]{1,2,0:T(8,128)(2,1)}), bf16[64,128,64]{1,2,0:T(8,128)(2,1)}, u32[]{:S(2)}, u32[]{:S(2)}) async-start(bf16[64,128,64]{1,2,0:T(8,128)(2,1)} %get-tuple-element.15), calls=%async_computation.1 | async-start | bytes 2097152 | tf_op jit(solution)/shard_map/all_to_all | solution.py:53
  45.0 73.4 %all-to-all-start = ((bf16[64,384,64]{1,2,0:T(8,128)(2,1)}), bf16[64,384,64]{1,2,0:T(8,128)(2,1)S(1)}, u32[]{:S(2)}, u32[]{:S(2)}) async-start(bf16[64,384,64]{1,2,0:T(8,128)(2,1)} %broadcast_select_fusion), calls=%async_computation | async-start | bytes 6291456 | tf_op jit(solution)/shard_map/all_to_all | solution.py:52
  52.2 119.0 %all-gather.8.cloned.1.call-start = ((), (), s32[]{:S(2)}) async-start(), calls=%async_computation.6 | async-start | bytes 3145728 | tf_op jit(solution)/shard_map/all_gather | solution.py:59
  57.5 155.3 %all-gather.6.cloned.1.call-start = ((), (), s32[]{:S(2)}) async-start(), calls=%async_computation.5 | async-start | bytes 9437184 | tf_op jit(solution)/shard_map/all_gather | solution.py:58
  128.8 1.2 copy-start.2
  159.5 9.1 %copy-start.4 = (s32[64]{0:T(128)S(1)}, s32[64]{0:T(128)}, u32[]{:S(2)}) copy-start(s32[64]{0:T(128)} %param.12) | copy-start | bytes 772
  159.5 456.2 %all-to-all-start.3 = ((bf16[64,32,3584]{2,1,0:T(8,128)(2,1)}), bf16[64,32,3584]{2,1,0:T(8,128)(2,1)}, u32[]{:S(2)}, u32[]{:S(2)}) async-start(bf16[64,32,3584]{2,1,0:T(8,128)(2,1)} %param.17), calls=%async_computation.3 | async-start | bytes 29360128 | tf_op jit(solution)/shard_map/all_to_all | solution.py:55
  167.9 417.5 %all-gather.10.cloned.1.call-start = ((), (), s32[]{:S(2)}) async-start(), calls=%async_computation.7 | async-start | bytes 10485760 | tf_op jit(solution)/shard_map/all_gather | solution.py:69
  168.6 44.2 %copy-start.5 = (bf16[64,1536]{1,0:T(8,128)(2,1)S(1)}, bf16[64,1536]{1,0:T(8,128)(2,1)}, u32[]{:S(2)}) copy-start(bf16[64,1536]{1,0:T(8,128)(2,1)} %param.10) | copy-start | bytes 589828
  168.6 460.7 %all-gather.14.cloned.1.call-start = ((), (), s32[]{:S(2)}) async-start(), calls=%async_computation.9 | async-start | bytes 3145728 | tf_op jit(solution)/shard_map/all_gather | solution.py:60
  170.9 485.3 %all-gather.12.cloned.1.call-start = ((), (), s32[]{:S(2)}) async-start(), calls=%async_computation.8 | async-start | bytes 3145728 | tf_op jit(solution)/shard_map/all_gather | solution.py:82
  585.4 7.9 %copy-start.3 = (bf16[64,128,512]{2,1,0:T(8,128)(2,1)S(1)}, bf16[64,128,512]{2,1,0:T(8,128)(2,1)}, u32[]{:S(2)}) copy-start(bf16[64,128,512]{2,1,0:T(8,128)(2,1)} %all-gather.10.cloned.1.call-done) | copy-start | bytes 25165828
  598.1 126.9 %reduce-scatter.2.cloned.1.call-start = ((), (), s32[]{:S(2)}) async-start(), calls=%async_computation.10 | async-start | bytes 2064384 | tf_op jit(solution)/shard_map/reduce_scatter | solution.py:83
  656.3 70.2 %copy-start.1 = (bf16[64,384,64]{1,2,0:T(8,128)(2,1)S(1)}, bf16[64,384,64]{1,2,0:T(8,128)(2,1)}, u32[]{:S(2)}) copy-start(bf16[64,384,64]{1,2,0:T(8,128)(2,1)} %param.14) | copy-start | bytes 9437188
Sparse Core Ops, SparseCore 0:
  57.7 35.0 all-gather.7
  128.9 83.8 all-gather.5
  214.4 370.9 all-gather.9
  586.8 34.9 all-gather.13
  623.1 33.1 all-gather.11
  695.6 29.2 reduce-scatter.1
where the time goes:
time: 742 us; the launch traced here: 733 us
  waiting for transfers between devices  551 us (74%)
  matrix products  64.5 us (9%)
  local copies, waits for them, and re-layouts  41.9 us (6%)
  blocking collectives  29.5 us (4%)
  starting transfers between devices  20.9 us (3%)
  between operations  13.6 us (2%)
  other arithmetic  11.5 us (2%)
    all_gather x1, waiting for transfers between devices, local(): piece = lax.all_gather(kv_cache, 'head', axis=0, tiled=True)  359 us
    all_to_all x1, waiting for transfers between devices, local(): lax.all_to_all(query_up, 'head', split_axis=0, concat_axis=1, tiled=True)  60.8 us
    all_gather x1, waiting for transfers between devices, local(): lax.all_gather(query_up, 'row', axis=2, tiled=True)  41.6 us
    dot_general x1, matrix products, local(): jnp.einsum('rhk,hko->ro', gathered, absorbed_o, preferred_element_type=jn...  39.2 us
    all_to_all x1, blocking collectives, local(): lax.all_to_all(value_up, 'head', split_axis=0, concat_axis=1, tiled=True)  29.5 us
    reduce_scatter x1, waiting for transfers between devices, local(): lax.psum_scatter(jnp.einsum('rhk,hko->ro', gathered, absorbed_o, preferre...  29.4 us
    all_gather x1, waiting for transfers between devices, local(): gathered = lax.all_gather(attended, 'row', axis=0, tiled=True)  27 us
    all_to_all x1, waiting for transfers between devices, local(): lax.all_to_all(out_stored, 'head', split_axis=0, concat_axis=1, tiled=True)  17.4 us
  transfers between devices with their start and end apart: 9, of which 7 were waited for; matrix products, arithmetic and copies ran while one was open for 7% of the time, Pallas kernels for 0%

commit v1 on v0

--- a/solution.py
+++ b/solution.py
@@ -1,8 +1,11 @@
+import functools
 import math
 
 import jax
 import jax.numpy as jnp
 from jax import lax
+from jax.experimental import pallas as pl
+from jax.experimental.pallas import tpu as pltpu
 from jax.sharding import PartitionSpec as P
 
 DH = 128
@@ -38,7 +41,7 @@
     return (newest, mass, accum)
 
 
-def local(
+def local_general(
     query_latent, kv_cache, row_lengths, head_map, uq_stored, uk_stored, uv_stored, out_stored
 ):
     slots = uq_stored.shape[0]
@@ -89,6 +92,373 @@
     return summed.astype(jnp.bfloat16)
 
 
+MESH = pl.DeviceIdType.MESH
+F32 = jnp.float32
+BF16 = jnp.bfloat16
+
+
+def attention_kernel(
+    n_row,
+    n_head,
+    scale,
+    ql_ref,
+    kv_ref,
+    mask_ref,
+    uq_ref,
+    uk_ref,
+    uv_ref,
+    v_out,
+    lat,
+    q_send,
+    q_recv,
+    uk_send,
+    uk_recv,
+    uv_send,
+    uv_recv,
+    wide,
+    x_send,
+    x_recv,
+    y_send,
+    y_recv,
+    v_send,
+    send_sem,
+    recv_sem,
+    own_sem,
+):
+    n = n_row * n_head
+    row = lax.axis_index("row")
+    head = lax.axis_index("head")
+    me = row * n_head + head
+    slots, part, half = uq_ref.shape
+    per = slots // n
+    pairs = per // 2
+    rows = ql_ref.shape[0]
+    batch = rows * n_row
+    own = batch // n
+    peers = [lax.rem(me + k, n) for k in range(1, n)]
+
+    def place(peer):
+        return {"row": peer // n_head, "head": lax.rem(peer, n_head)}
+
+    def remote(phase, k, src, dst, peer):
+        return pltpu.make_async_remote_copy(
+            src_ref=src,
+            dst_ref=dst,
+            send_sem=send_sem.at[phase, k],
+            recv_sem=recv_sem.at[phase, me],
+            device_id=place(peer),
+            device_id_type=MESH,
+        )
+
+    def arrival(phase, src, dst):
+        for k in range(1, n):
+            peer = lax.rem(me + k, n)
+            pltpu.make_async_remote_copy(
+                src_ref=src.at[peer],
+                dst_ref=dst.at[peer],
+                send_sem=send_sem.at[phase, k],
+                recv_sem=recv_sem.at[phase, peer],
+                device_id=place(peer),
+                device_id_type=MESH,
+            ).wait_recv()
+
+    def spread(phase, src, dst):
+        copies = []
+        for k in range(1, n):
+            peer = lax.rem(me + k, n)
+            copy = remote(phase, k, src.at[peer], dst.at[me], peer)
+            copy.start()
+            copies.append(copy)
+        return copies
+
+    barrier = pltpu.get_barrier_semaphore()
+    for peer in peers:
+        pl.semaphore_signal(barrier, inc=1, device_id=place(peer), device_id_type=MESH)
+    pl.semaphore_wait(barrier, n - 1)
+
+    columns = pl.ds(pl.multiple_of(head * part, 128), part)
+    pending = []
+    for k in range(1, n_row):
+        other = lax.rem(row + k, n_row)
+        copy = remote(0, k, ql_ref.at[:, columns], lat.at[row], other * n_head + head)
+        copy.start()
+        pending.append(copy)
+    lat[row] = ql_ref[:, columns]
+
+    def pack(pair, carry):
+        peer = pair // pairs
+        at = lax.rem(pair, pairs)
+        uk_send[peer, at] = jnp.concatenate([uk_ref[2 * pair], uk_ref[2 * pair + 1]], axis=1)
+        uv_send[peer, at] = jnp.concatenate([uv_ref[2 * pair], uv_ref[2 * pair + 1]], axis=1)
+        return carry
+
+    lax.fori_loop(0, slots // 2, pack, 0)
+
+    for k in range(1, n_row):
+        other = lax.rem(row + k, n_row)
+        pltpu.make_async_remote_copy(
+            src_ref=lat.at[other],
+            dst_ref=lat.at[other],
+            send_sem=send_sem.at[0, k],
+            recv_sem=recv_sem.at[0, other * n_head + head],
+            device_id=place(other * n_head + head),
+            device_id_type=MESH,
+        ).wait_recv()
+    latent = lat[...].reshape(batch, part)
+
+    for k in range(1, n + 1):
+        peer = lax.rem(me + k, n)
+        for at in range(pairs):
+            slot = peer * per + 2 * at
+            first = jnp.dot(latent, uq_ref[slot], preferred_element_type=F32)
+            second = jnp.dot(latent, uq_ref[slot + 1], preferred_element_type=F32)
+            both = jnp.concatenate([first, second], axis=1).astype(BF16)
+            if k < n:
+                q_send[peer, at] = both
+            else:
+                q_recv[me, at] = both
+        if k < n:
+            copy = remote(1, k, q_send.at[peer], q_recv.at[me], peer)
+            copy.start()
+            pending.append(copy)
+    pending += spread(2, uk_send, uk_recv)
+    uk_recv[me] = uk_send[me]
+    uv_recv[me] = uv_send[me]
+
+    arrival(1, q_send, q_recv)
+    arrival(2, uk_send, uk_recv)
+
+    def joined(ref, at, which):
+        blocks = []
+        for r in range(n_row):
+            block = ref[r * n_head : (r + 1) * n_head, at]
+            block = block.reshape(-1, block.shape[-1])
+            blocks.append(block[:, which * half : (which + 1) * half])
+        return jnp.concatenate(blocks, axis=1)
+
+    for at in range(pairs):
+        sums = []
+        for r in range(n_row):
+            total = q_recv[r * n_head, at].astype(F32)
+            for h in range(1, n_head):
+                total = total + q_recv[r * n_head + h, at].astype(F32)
+            sums.append(total.astype(BF16))
+        for which in range(2):
+            query = jnp.concatenate([s[:, which * half : (which + 1) * half] for s in sums], axis=1)
+            key_up = joined(uk_recv, at, which)
+            wide[:, 2 * at + which, :] = lax.dot_general(
+                query, key_up, (((1,), (1,)), ((), ())), preferred_element_type=F32
+            )
+    for k in range(1, n + 1):
+        peer = lax.rem(me + k, n)
+        block = wide[pl.ds(peer * own, own)].reshape(own * per, -1).astype(BF16)
+        if k < n:
+            x_send[peer] = block
+            copy = remote(3, k, x_send.at[peer], x_recv.at[me], peer)
+            copy.start()
+            pending.append(copy)
+        else:
+            x_recv[me] = block
+    pending += spread(4, uv_send, uv_recv)
+    arrival(3, x_send, x_recv)
+
+    for b in range(own):
+        query = jnp.concatenate(
+            [x_recv[p].astype(F32)[b * per : (b + 1) * per] for p in range(n)], axis=0
+        ).astype(BF16)
+        cache = kv_ref[b]
+        scores = (
+            lax.dot_general(query, cache, (((1,), (1,)), ((), ())), preferred_element_type=F32)
+            * scale
+        )
+        alive = mask_ref[b : b + 1, :] > 0
+        scores = jnp.where(alive, scores, -1e30)
+        top = jnp.max(scores, axis=1, keepdims=True)
+        weights = jnp.where(alive, jnp.exp(scores - top), 0.0)
+        mass = jnp.sum(weights, axis=1, keepdims=True)
+        mixed = jnp.dot(weights.astype(BF16), cache, preferred_element_type=F32) / mass
+        for p in range(n):
+            wide[p * own + b] = mixed[p * per : (p + 1) * per]
+    for k in range(1, n + 1):
+        peer = lax.rem(me + k, n)
+        block = wide[pl.ds(peer * own, own)].reshape(own * per, -1).astype(BF16)
+        if k < n:
+            y_send[peer] = block
+            copy = remote(5, k, y_send.at[peer], y_recv.at[me], peer)
+            copy.start()
+            pending.append(copy)
+        else:
+            y_recv[me] = block
+    arrival(4, uv_send, uv_recv)
+    arrival(5, y_send, y_recv)
+
+    wide[...] = y_recv[...].astype(F32).reshape(wide.shape)
+    values = []
+    for at in range(pairs):
+        for which in range(2):
+            mixed = wide[:, 2 * at + which, :].astype(BF16)
+            values.append(
+                jnp.dot(mixed, joined(uv_recv, at, which), preferred_element_type=F32).astype(BF16)
+            )
+    share = values[0].shape[1] // n_head
+    for h in range(n_head):
+        v_send[h] = jnp.concatenate([v[:, h * share : (h + 1) * share] for v in values], axis=1)
+    for k in range(1, n):
+        peer = lax.rem(me + k, n)
+        copy = remote(6, k, v_send.at[lax.rem(peer, n_head)], v_out.at[me], peer)
+        copy.start()
+        pending.append(copy)
+    v_out[me] = v_send[head]
+    arrival(6, v_out, v_out)
+    for copy in pending:
+        copy.wait_send()
+
+
+def sum_kernel(n_head, n_sub, part_ref, out_ref, recv, send_sem, recv_sem):
+    n = n_head * n_sub
+    me = lax.axis_index("head") * n_sub + lax.axis_index("sub")
+    own = out_ref.shape[0]
+
+    def place(peer):
+        return {"head": peer // n_sub, "sub": lax.rem(peer, n_sub)}
+
+    barrier = pltpu.get_barrier_semaphore()
+    for k in range(1, n):
+        pl.semaphore_signal(
+            barrier, inc=1, device_id=place(lax.rem(me + k, n)), device_id_type=MESH
+        )
+    pl.semaphore_wait(barrier, n - 1)
+    copies = []
+    for k in range(1, n):
+        peer = lax.rem(me + k, n)
+        copy = pltpu.make_async_remote_copy(
+            src_ref=part_ref.at[peer],
+            dst_ref=recv.at[me],
+            send_sem=send_sem.at[k],
+            recv_sem=recv_sem.at[me],
+            device_id=place(peer),
+            device_id_type=MESH,
+        )
+        copy.start()
+        copies.append(copy)
+    total = part_ref[me].astype(F32)
+    for k in range(1, n):
+        peer = lax.rem(me + k, n)
+        pltpu.make_async_remote_copy(
+            src_ref=part_ref.at[peer],
+            dst_ref=recv.at[peer],
+            send_sem=send_sem.at[k],
+            recv_sem=recv_sem.at[peer],
+            device_id=place(peer),
+            device_id_type=MESH,
+        ).wait_recv()
+        total = total + recv[peer].astype(F32)
+    out_ref[...] = total.astype(out_ref.dtype)
+    for copy in copies:
+        copy.wait_send()
+
+
+def local_fast(
+    n_row,
+    n_head,
+    n_sub,
+    query_latent,
+    kv_cache,
+    row_lengths,
+    head_map,
+    uq_stored,
+    uk_stored,
+    uv_stored,
+    out_stored,
+):
+    n = n_row * n_head
+    slots, part, half = uq_stored.shape
+    own, width, latent = kv_cache.shape
+    rows = query_latent.shape[0]
+    batch = rows * n_row
+    per = slots // n
+    k_part = uk_stored.shape[1]
+    depth = half * n_row
+    share = depth // n_head
+    lengths = lax.dynamic_slice_in_dim(row_lengths, lax.axis_index("head") * own, own, 0)
+    mask = (jnp.arange(width, dtype=jnp.int32)[None, :] < lengths[:, None]).astype(jnp.int32)
+    vmem = pl.BlockSpec(memory_space=pltpu.VMEM)
+    values = pl.pallas_call(
+        functools.partial(attention_kernel, n_row, n_head, 1.0 / math.sqrt(DH)),
+        out_shape=jax.ShapeDtypeStruct((n, batch, per * share), BF16),
+        in_specs=[vmem] * 6,
+        out_specs=vmem,
+        scratch_shapes=[
+            pltpu.VMEM((n_row, rows, part), BF16),
+            pltpu.VMEM((n, per // 2, batch, 2 * half), BF16),
+            pltpu.VMEM((n, per // 2, batch, 2 * half), BF16),
+            pltpu.VMEM((n, per // 2, k_part, 2 * half), BF16),
+            pltpu.VMEM((n, per // 2, k_part, 2 * half), BF16),
+            pltpu.VMEM((n, per // 2, k_part, 2 * half), BF16),
+            pltpu.VMEM((n, per // 2, k_part, 2 * half), BF16),
+            pltpu.VMEM((batch, per, latent), F32),
+            pltpu.VMEM((n, own * per, latent), BF16),
+            pltpu.VMEM((n, own * per, latent), BF16),
+            pltpu.VMEM((n, own * per, latent), BF16),
+            pltpu.VMEM((n, own * per, latent), BF16),
+            pltpu.VMEM((n_head, batch, per * share), BF16),
+            pltpu.SemaphoreType.DMA((7, n)),
+            pltpu.SemaphoreType.DMA((7, n)),
+            pltpu.SemaphoreType.DMA,
+        ],
+        compiler_params=pltpu.CompilerParams(
+            collective_id=0, has_side_effects=True, vmem_limit_bytes=56 * 1024 * 1024
+        ),
+    )(query_latent, kv_cache, mask, uq_stored, uk_stored, uv_stored)
+    first_slot = lax.axis_index("sub") * slots
+    local_map = lax.dynamic_slice_in_dim(head_map, first_slot, slots, 0)
+    slot_order = jnp.argsort(local_map)
+    values = values.reshape(n, batch, per, share).transpose(0, 2, 1, 3)
+    values = jnp.take(values.reshape(slots, batch, share), slot_order, axis=0)
+    values = values.transpose(1, 0, 2).reshape(batch, slots * share)
+    partial = jnp.dot(
+        values, out_stored.reshape(slots * share, -1), preferred_element_type=F32
+    ).astype(BF16)
+    peers = n_head * n_sub
+    partial = partial.reshape(peers, batch // peers, -1)
+    return pl.pallas_call(
+        functools.partial(sum_kernel, n_head, n_sub),
+        out_shape=jax.ShapeDtypeStruct(partial.shape[1:], BF16),
+        in_specs=[vmem],
+        out_specs=vmem,
+        scratch_shapes=[
+            pltpu.VMEM(partial.shape, BF16),
+            pltpu.SemaphoreType.DMA((peers,)),
+            pltpu.SemaphoreType.DMA((peers,)),
+        ],
+        compiler_params=pltpu.CompilerParams(
+            collective_id=1, has_side_effects=True, vmem_limit_bytes=32 * 1024 * 1024
+        ),
+    )(partial)
+
+
+def choose_local(mesh):
+    n_row, n_head, n_sub = mesh.shape["row"], mesh.shape["head"], mesh.shape["sub"]
+
+    def local(query_latent, kv_cache, row_lengths, head_map, uq, uk, uv, out_stored):
+        args = (query_latent, kv_cache, row_lengths, head_map, uq, uk, uv, out_stored)
+        n = n_row * n_head
+        batch = query_latent.shape[0] * n_row
+        fits = (
+            uq.shape[0] % (8 * n) == 0
+            and uq.shape[1] % 128 == 0
+            and uk.shape[1] % 128 == 0
+            and uq.shape[2] % 64 == 0
+            and batch % (16 * n) == 0
+            and batch % (16 * n_head * n_sub) == 0
+        )
+        if fits:
+            return local_fast(n_row, n_head, n_sub, *args)
+        return local_general(*args)
+
+    return local
+
+
 def solution(mesh):
     in_specs = (
         P(("group", "row"), None),
@@ -101,4 +471,5 @@
         P("sub", "head", "row"),
     )
     out_specs = P(("group", "head", "sub"), "row")
+    local = choose_local(mesh)
     return jax.shard_map(local, mesh=mesh, in_specs=in_specs, out_specs=out_specs, check_vma=False)

time: 742 us -> 193 us (0.26); the launches traced: 733 us -> 193 us
  waiting for transfers between devices: 551 us -> 0 us
  Pallas kernels: 0 us -> 169 us
  matrix products: 64.5 us -> 7.34 us
  blocking collectives: 29.5 us -> 0 us
  local copies, waits for them, and re-layouts: 41.9 us -> 13.7 us
  starting transfers between devices: 20.9 us -> 0 us
  between operations: 13.6 us -> 0.06 us
  other arithmetic: 11.5 us -> 2.73 us
    all_gather x5 -> x0, waiting for transfers between devices: 428 us -> none  [the longest x1 359 us: local(): piece = lax.all_gather(kv_cache, 'head', axis=0, tiled=True)]
    pallas_call x0 -> x2, Pallas kernels: none -> 169 us  [the longest x1 142 us: local_fast(): pl.pallas_call(functools.partial(attention_kernel, n_row, n_head, 1.0 / m...]
    all_to_all x3 -> x0, waiting for transfers between devices: 93.5 us -> none  [the longest x1 60.8 us: local(): lax.all_to_all(query_up, 'head', split_axis=0, concat_axis=1, tiled=True)]
    dot_general x6 -> x1, matrix products: 64.5 us -> 7.34 us  [local_fast(): jnp.dot(values, out_stored.reshape(slots * share, -1), preferred_element_...]
    all_to_all x7 -> x0, local copies, waits for them, and re-layouts: 31.4 us -> none  [the longest x1 13.6 us: local(): lax.all_to_all(out_stored, 'head', split_axis=0, concat_axis=1, tiled=True)]
    all_to_all x1 -> x0, blocking collectives: 29.5 us -> none  [local(): lax.all_to_all(value_up, 'head', split_axis=0, concat_axis=1, tiled=True)]
    reduce_scatter x1 -> x0, waiting for transfers between devices: 29.4 us -> none  [local(): lax.psum_scatter(jnp.einsum('rhk,hko->ro', gathered, absorbed_o, preferre...]
    all_to_all x3 -> x0, starting transfers between devices: 20.3 us -> none  [the longest x1 8.35 us: local(): lax.all_to_all(out_stored, 'head', split_axis=0, concat_axis=1, tiled=True)]
  transfers between devices with their start and end apart: 9 -> 0, of which waited for: 7 -> 0; matrix products, arithmetic and copies ran while one was open for 7% -> 0% of each run, Pallas kernels for 0% -> 0%
where the time goes in v1:
time: 193 us
  Pallas kernels  169 us (88%)
  local copies, waits for them, and re-layouts  13.7 us (7%)
  matrix products  7.34 us (4%)
  other arithmetic  2.73 us (1%)
    pallas_call x1, Pallas kernels, local_fast(): pl.pallas_call(functools.partial(attention_kernel, n_row, n_head, 1.0 / m...  142 us
    pallas_call x1, Pallas kernels, local_fast(): pl.pallas_call(functools.partial(sum_kernel, n_head, n_sub), out_shape=ja...  26.8 us
    unnamed x10, local copies, waits for them, and re-layouts  10.9 us
    dot_general x1, matrix products, local_fast(): jnp.dot(values, out_stored.reshape(slots * share, -1), preferred_element_...  7.34 us

profile of v1, /device:TPU:13, one launch (start us, length us, event | category | flops | bytes accessed | tf_op | source)
XLA Modules:
  0.0 192.6 jit_solution(4177650847801664637)
XLA Ops:
  0.0 0.7 dynamic_slice.7
  0.7 0.7 fusion.5.mask_ref
  1.4 0.0 copy-start
  1.4 6.6 %copy.13.uq_ref = bf16[64,384,64]{2,1,0:T(8,128)(2,1)} copy(bf16[64,384,64]{1,2,0:T(8,128)(2,1)} %param.12) | data formatting | bytes 6291456 | tf_op args[4]
  8.0 0.0 copy-done
  8.0 0.0 copy-start.1
  8.0 1.8 copy.14.uk_ref
  9.8 0.0 copy-done.1
  9.8 1.8 copy.15.uv_ref
  11.6 0.0 copy-start.2
  11.6 142.0 %shard_map.82 = bf16[8,128,256]{2,1,0:T(8,128)(2,1)} custom-call(bf16[64,1536]{1,0:T(8,128)(2,1)} %ql_ref.1, bf16[16,128,512]{2,1,0:T(8,128)(2,1)} %kv_ref.1, s32[16,128]{1,0:T(8,128)} %fusion.5.mask_ref, bf16[64,384,64]{2,1,0:T(8,128)(2,1)} %copy.13.uq_ref, bf16[64,128,64]{2,1,0:T(8,128)(2,1)} %copy.14.uk_ref, bf16[64,128,64]{2,1,0:T(8,128)(2,1)} %copy.15.uv_ref), custom_call_target="tpu_custom_call" | custom-call | tf_op jit(solution)/shard_map/pallas_call | solution.py:386
  153.7 1.3 copy.16
  155.0 0.0 copy-done.2
  155.0 0.1 dynamic_slice.6
  155.1 2.0 %sort.17 = (s32[64]{0:T(128)}, s32[64]{0:T(128)S(1)}) sort(s32[64]{0:T(128)S(1)} %dynamic_slice.6, s32[64]{0:T(128)S(1)} %iota.8), dimensions={0}, to_apply=%region_0.0 | sort | flops 384 | bytes 1024 | tf_op jit(solution)/shard_map/jit(argsort)/sort | solution.py:415
  157.1 0.7 gather_fusion
  157.8 7.3 %fusion = bf16[128,3584]{1,0:T(8,128)(2,1)S(1)} fusion(bf16[64,32,3584]{2,1,0:T(8,128)(2,1)} %param.15, bf16[64,128,32]{1,2,0:T(8,128)(2,1)S(1)} %gather_fusion, pred[64]{0:T(512)(128)(4,1)S(1)} %compare_and_fusion), kind=kOutput, calls=%fused_computation.2 | convolution fusion | flops 1879769088 | bytes 16121920 | tf_op jit(solution)/shard_map/dot_general | solution.py:419
  165.2 26.8 %shard_map.83 = bf16[16,3584]{1,0:T(8,128)(2,1)S(1)} custom-call(bf16[8,16,3584]{2,1,0:T(8,128)(2,1)S(1)} %bitcast.14), custom_call_target="tpu_custom_call" | custom-call | tf_op jit(solution)/shard_map/pallas_call | solution.py:424
  192.0 0.6 copy.22
  (4 shorter events, 0.0 us)
Async XLA Ops:
  1.4 6.6 %copy-start = (bf16[64,128,64]{1,2,0:T(8,128)(2,1)S(1)}, bf16[64,128,64]{1,2,0:T(8,128)(2,1)}, u32[]{:S(2)}) copy-start(bf16[64,128,64]{1,2,0:T(8,128)(2,1)} %param.13) | copy-start | bytes 3145732
  8.0 1.8 copy-start.1
  11.6 143.4 %copy-start.2 = (s32[128]{0:T(128)S(1)}, s32[128]{0:T(128)}, u32[]{:S(2)}) copy-start(s32[128]{0:T(128)} %param.11) | copy-start | bytes 1540

commit v2 on v0

--- a/solution.py
+++ b/solution.py
@@ -1,8 +1,11 @@
+import functools
 import math
 
 import jax
 import jax.numpy as jnp
 from jax import lax
+from jax.experimental import pallas as pl
+from jax.experimental.pallas import tpu as pltpu
 from jax.sharding import PartitionSpec as P
 
 DH = 128
@@ -38,7 +41,7 @@
     return (newest, mass, accum)
 
 
-def local(
+def local_general(
     query_latent, kv_cache, row_lengths, head_map, uq_stored, uk_stored, uv_stored, out_stored
 ):
     slots = uq_stored.shape[0]
@@ -89,6 +92,461 @@
     return summed.astype(jnp.bfloat16)
 
 
+MESH = pl.DeviceIdType.MESH
+F32 = jnp.float32
+BF16 = jnp.bfloat16
+
+
+def attention_kernel(
+    n_row,
+    n_head,
+    scale,
+    ql_ref,
+    kv_ref,
+    mask_ref,
+    map_ref,
+    uq_ref,
+    uk_ref,
+    uv_ref,
+    out_hbm,
+    result,
+    lat,
+    q_send,
+    q_recv,
+    uk_recv,
+    uv_recv,
+    wide,
+    x_send,
+    x_recv,
+    y_send,
+    y_recv,
+    v_send,
+    v_recv,
+    pick,
+    picked,
+    out_up,
+    part_sums,
+    near_sums,
+    chip_sums,
+    far_sums,
+    send_sem,
+    recv_sem,
+    load_sem,
+):
+    n = n_row * n_head
+    group = lax.axis_index("group")
+    sub = lax.axis_index("sub")
+    row = lax.axis_index("row")
+    head = lax.axis_index("head")
+    me = row * n_head + head
+    slots, half, part = uq_ref.shape
+    per = slots // n
+    pairs = per // 2
+    rows = ql_ref.shape[0]
+    batch = rows * n_row
+    own = batch // n
+    near = own // 2
+    kept = pl.ds(group * (per // 2), per // 2)
+    turns = [n_head // 2] + [d for d in range(1, n_head) if d != n_head // 2] + [0]
+    shifts = [(dr, dh) for dh in turns for dr in range(n_row) if (dr, dh) != (0, 0)]
+    peers = [
+        lax.rem(row + dr, n_row) * n_head + lax.rem(head + dh, n_head) for dr, dh in shifts
+    ]
+    pending = []
+
+    def place(peer):
+        return {"row": peer // n_head, "head": lax.rem(peer, n_head)}
+
+    def remote(phase, k, src, dst, slot, device):
+        return pltpu.make_async_remote_copy(
+            src_ref=src,
+            dst_ref=dst,
+            send_sem=send_sem.at[phase, k],
+            recv_sem=recv_sem.at[phase, slot],
+            device_id=device,
+            device_id_type=MESH,
+        )
+
+    def send(phase, k, src, dst, peer):
+        copy = remote(phase, k, src, dst, me, place(peer))
+        copy.start()
+        pending.append(copy)
+
+    def arrived(phase, k, dst, peer):
+        remote(phase, k, dst, dst, peer, place(peer)).wait_recv()
+
+    def send_weights(phase, src, dst):
+        for k, peer in enumerate(peers):
+            first = peer * per + group * (per // 2)
+            send(phase, k, src.at[pl.ds(first, per // 2)], dst.at[me, kept], peer)
+
+    def pass_weights(phase, dst):
+        for k, peer in enumerate(peers):
+            arrived(phase, k, dst.at[peer, kept], peer)
+            block = dst.at[peer, kept]
+            copy = remote(phase + 1, k, block, block, peer, {"group": 1 - group})
+            copy.start()
+            pending.append(copy)
+
+    def await_weights(phase, dst):
+        other = pl.ds((1 - group) * (per // 2), per // 2)
+        for k, peer in enumerate(peers):
+            block = dst.at[peer, other]
+            remote(phase + 1, k, block, block, peer, {"group": 1 - group}).wait_recv()
+
+    barrier = pltpu.get_barrier_semaphore()
+    for peer in peers:
+        pl.semaphore_signal(barrier, inc=1, device_id=place(peer), device_id_type=MESH)
+    pl.semaphore_signal(barrier, inc=1, device_id={"group": 1 - group}, device_id_type=MESH)
+    pl.semaphore_signal(barrier, inc=1, device_id={"sub": 1 - sub}, device_id_type=MESH)
+    pl.semaphore_wait(barrier, n + 1)
+
+    columns = pl.ds(pl.multiple_of(head * part, 128), part)
+    others = [lax.rem(row + k, n_row) for k in range(1, n_row)]
+    for k, other in enumerate(others):
+        send(0, k, ql_ref.at[:, columns], lat.at[row], other * n_head + head)
+    send_weights(2, uk_ref, uk_recv)
+    load = pltpu.make_async_copy(out_hbm, out_up, load_sem)
+    load.start()
+    lat[row] = ql_ref[:, columns]
+    mine = pl.ds(me * per, per)
+    uk_recv[me] = uk_ref[mine]
+    uv_recv[me] = uv_ref[mine]
+    for k, other in enumerate(others):
+        arrived(0, k, lat.at[other], other * n_head + head)
+    latent = lat[...].reshape(batch, part)
+
+    for k, peer in enumerate(peers + [me]):
+        for at in range(pairs):
+            two = uq_ref[pl.ds(peer * per + 2 * at, 2)].reshape(2 * half, part)
+            both = lax.dot_general(
+                latent, two, (((1,), (1,)), ((), ())), preferred_element_type=F32
+            ).astype(BF16)
+            if k < n - 1:
+                q_send[peer, at] = both
+            else:
+                q_recv[me, at] = both
+        if k < n - 1:
+            send(1, k, q_send.at[peer], q_recv.at[me], peer)
+    send_weights(8, uv_ref, uv_recv)
+    pass_weights(2, uk_recv)
+
+    share = out_hbm.shape[1]
+    spots = lax.broadcasted_iota(jnp.int32, (share, slots * share), 1)
+    spots = spots - lax.broadcasted_iota(jnp.int32, (share, slots * share), 0)
+
+    def mark(slot, carry):
+        lanes = spots == map_ref[slot] * share
+        first = pl.multiple_of(slot * share, share)
+        pick[pl.ds(first, share), :] = jnp.where(lanes, 1.0, 0.0).astype(BF16)
+        return carry
+
+    lax.fori_loop(0, slots, mark, 0)
+
+    for k, peer in enumerate(peers):
+        arrived(1, k, q_recv.at[peer], peer)
+    queries = []
+    for at in range(pairs):
+        sums = []
+        for r in range(n_row):
+            total = q_recv[r * n_head, at].astype(F32)
+            for h in range(1, n_head):
+                total = total + q_recv[r * n_head + h, at].astype(F32)
+            sums.append(total.astype(BF16))
+        for which in range(2):
+            queries.append(
+                jnp.concatenate([s[:, which * half : (which + 1) * half] for s in sums], axis=1)
+            )
+    await_weights(2, uk_recv)
+
+    def joined(ref, slot):
+        return jnp.concatenate(
+            [
+                jnp.concatenate([ref[r * n_head + h, slot] for h in range(n_head)], axis=1)
+                for r in range(n_row)
+            ],
+            axis=0,
+        )
+
+    for slot in range(per):
+        wide[:, slot, :] = jnp.dot(
+            queries[slot], joined(uk_recv, slot), preferred_element_type=F32
+        )
+    for part_at in range(2):
+        for k, peer in enumerate(peers + [me]):
+            block = wide[pl.ds(peer * own + part_at * near, near)]
+            block = block.reshape(near * per, -1).astype(BF16)
+            if k < n - 1:
+                x_send[part_at, peer] = block
+                send(
+                    4 + part_at, k, x_send.at[part_at, peer], x_recv.at[part_at, me], peer
+                )
+            else:
+                x_recv[part_at, me] = block
+    pass_weights(8, uv_recv)
+
+    for part_at in range(2):
+        for k, peer in enumerate(peers):
+            arrived(4 + part_at, k, x_recv.at[part_at, peer], peer)
+        wanted = x_recv[part_at].astype(F32)
+        scores = []
+        for b in range(near):
+            query = wanted[:, b * per : (b + 1) * per].reshape(slots, -1).astype(BF16)
+            score = (
+                lax.dot_general(
+                    query,
+                    kv_ref[part_at * near + b],
+                    (((1,), (1,)), ((), ())),
+                    preferred_element_type=F32,
+                )
+                * scale
+            )
+            at = part_at * near + b
+            scores.append(jnp.where(mask_ref[at : at + 1, :] > 0, score, -1e30))
+        stacked = jnp.concatenate(scores, axis=0)
+        top = jnp.max(stacked, axis=1, keepdims=True)
+        weights = jnp.exp(stacked - top)
+        mass = jnp.sum(weights, axis=1, keepdims=True)
+        weights = (weights / mass).astype(BF16)
+        for b in range(near):
+            mixed = jnp.dot(
+                weights[b * slots : (b + 1) * slots],
+                kv_ref[part_at * near + b],
+                preferred_element_type=F32,
+            )
+            for p in range(n):
+                wide[p * own + part_at * near + b] = mixed[p * per : (p + 1) * per]
+        for k, peer in enumerate(peers + [me]):
+            block = wide[pl.ds(peer * own + part_at * near, near)]
+            block = block.reshape(near * per, -1).astype(BF16)
+            if k < n - 1:
+                y_send[part_at, peer] = block
+                send(
+                    6 + part_at, k, y_send.at[part_at, peer], y_recv.at[part_at, me], peer
+                )
+            else:
+                y_recv[part_at, me] = block
+    await_weights(8, uv_recv)
+    for part_at in range(2):
+        for k, peer in enumerate(peers):
+            arrived(6 + part_at, k, y_recv.at[part_at, peer], peer)
+        for p in range(n):
+            first = p * own + part_at * near
+            wide[first : first + near] = (
+                y_recv[part_at, p].astype(F32).reshape(near, per, wide.shape[2])
+            )
+    values = []
+    for slot in range(per):
+        values.append(
+            lax.dot_general(
+                wide[:, slot, :].astype(BF16),
+                joined(uv_recv, slot),
+                (((1,), (1,)), ((), ())),
+                preferred_element_type=F32,
+            ).astype(BF16)
+        )
+    for h in range(n_head):
+        v_send[h] = jnp.concatenate([v[:, h * share : (h + 1) * share] for v in values], axis=1)
+    heads = [lax.rem(head + d, n_head) for d in turns]
+    v_recv[me] = v_send[head]
+    for k, other in enumerate(heads[:-1]):
+        send(10, k, v_send.at[other], v_recv.at[me], row * n_head + other)
+
+    def forward(k, peer):
+        for i, other in enumerate(others):
+            copy = remote(
+                11,
+                k * (n_row - 1) + i,
+                v_recv.at[peer],
+                v_recv.at[peer],
+                peer,
+                place(other * n_head + head),
+            )
+            copy.start()
+            pending.append(copy)
+
+    deep = per * share
+
+    def spread(peer, fresh):
+        rows_of = pl.ds(pl.multiple_of(peer * deep, deep), deep)
+        term = jnp.dot(v_recv[peer], pick[rows_of, :], preferred_element_type=F32)
+        picked[...] = term if fresh else picked[...] + term
+
+    forward(n_head - 1, me)
+    spread(me, True)
+    for k, other in enumerate(heads[:-1]):
+        peer = row * n_head + other
+        arrived(10, k, v_recv.at[peer], peer)
+        forward(k, peer)
+        spread(peer, False)
+    for i, away in enumerate(others):
+        for k, other in enumerate([heads[-1]] + heads[:-1]):
+            peer = away * n_head + other
+            remote(
+                11, 0, v_recv.at[peer], v_recv.at[peer], peer, place(away * n_head + head)
+            ).wait_recv()
+            spread(peer, False)
+
+    load.wait()
+    chunks, step = part_sums.shape[0], part_sums.shape[-1]
+    twin = {"sub": 1 - sub}
+    final = picked[...].astype(BF16)
+
+    def chip_copy(c):
+        return remote(12, c, part_sums.at[c, 1 - sub], near_sums.at[c], c, twin)
+
+    def head_copy(c, k, other):
+        return remote(
+            13 + c,
+            k,
+            chip_sums.at[c, other],
+            far_sums.at[c, head],
+            head,
+            {"head": other},
+        )
+
+    def add_chip(c):
+        chip_copy(c).wait_recv()
+        chip_sums[c] = (part_sums[c, sub].astype(F32) + near_sums[c].astype(F32)).astype(BF16)
+        for k, other in enumerate(heads[:-1]):
+            copy = head_copy(c, k, other)
+            copy.start()
+            pending.append(copy)
+
+    for c in range(chunks):
+        weights = out_up[:, :, c * step : (c + 1) * step].reshape(slots * share, step)
+        sums = jnp.dot(final, weights, preferred_element_type=F32).astype(BF16)
+        part_sums[c, 0] = sums.reshape(n_head, 2, -1, step)[:, 0]
+        part_sums[c, 1] = sums.reshape(n_head, 2, -1, step)[:, 1]
+        copy = chip_copy(c)
+        copy.start()
+        pending.append(copy)
+        if c > 0:
+            add_chip(c - 1)
+    add_chip(chunks - 1)
+    for c in range(chunks):
+        total = chip_sums[c, head].astype(F32)
+        for k, other in enumerate(heads[:-1]):
+            remote(
+                13 + c,
+                k,
+                chip_sums.at[c, other],
+                far_sums.at[c, other],
+                other,
+                {"head": other},
+            ).wait_recv()
+            total = total + far_sums[c, other].astype(F32)
+        result[:, c * step : (c + 1) * step] = total.astype(BF16)
+    for copy in pending:
+        copy.wait_send()
+
+
+def local_fast(
+    n_row,
+    n_head,
+    n_sub,
+    query_latent,
+    kv_cache,
+    row_lengths,
+    head_map,
+    uq_stored,
+    uk_stored,
+    uv_stored,
+    out_stored,
+):
+    n = n_row * n_head
+    slots, part, half = uq_stored.shape
+    own, width, latent = kv_cache.shape
+    rows = query_latent.shape[0]
+    batch = rows * n_row
+    per = slots // n
+    k_part = uk_stored.shape[1]
+    share = out_stored.shape[1]
+    wide_out = out_stored.shape[2]
+    chunks = 4
+    first_slot = lax.axis_index("sub") * slots
+    local_map = lax.dynamic_slice_in_dim(head_map, first_slot, slots, 0) - first_slot
+    lengths = lax.dynamic_slice_in_dim(row_lengths, lax.axis_index("head") * own, own, 0)
+    mask = (jnp.arange(width, dtype=jnp.int32)[None, :] < lengths[:, None]).astype(jnp.int32)
+    vmem = pl.BlockSpec(memory_space=pltpu.VMEM)
+    piece = pltpu.VMEM((2, n, own // 2 * per, latent), BF16)
+    sums = pltpu.VMEM((chunks, n_head, batch // (n_head * n_sub), wide_out // chunks), BF16)
+    return pl.pallas_call(
+        functools.partial(attention_kernel, n_row, n_head, 1.0 / math.sqrt(DH)),
+        out_shape=jax.ShapeDtypeStruct((batch // (n_head * n_sub), wide_out), BF16),
+        in_specs=[vmem] * 3
+        + [pl.BlockSpec(memory_space=pltpu.SMEM)]
+        + [vmem] * 3
+        + [pl.BlockSpec(memory_space=pl.ANY)],
+        out_specs=vmem,
+        scratch_shapes=[
+            pltpu.VMEM((n_row, rows, part), BF16),
+            pltpu.VMEM((n, per // 2, batch, 2 * half), BF16),
+            pltpu.VMEM((n, per // 2, batch, 2 * half), BF16),
+            pltpu.VMEM((n, per, half, k_part), BF16),
+            pltpu.VMEM((n, per, half, k_part), BF16),
+            pltpu.VMEM((batch, per, latent), F32),
+            piece,
+            piece,
+            piece,
+            piece,
+            pltpu.VMEM((n_head, batch, per * share), BF16),
+            pltpu.VMEM((n, batch, per * share), BF16),
+            pltpu.VMEM((slots * share, slots * share), BF16),
+            pltpu.VMEM((batch, slots * share), F32),
+            pltpu.VMEM(out_stored.shape, BF16),
+            pltpu.VMEM((chunks, n_sub) + sums.shape[1:], BF16),
+            sums,
+            sums,
+            sums,
+            pltpu.SemaphoreType.DMA((13 + chunks, n)),
+            pltpu.SemaphoreType.DMA((13 + chunks, n)),
+            pltpu.SemaphoreType.DMA,
+        ],
+        compiler_params=pltpu.CompilerParams(
+            collective_id=0, has_side_effects=True, vmem_limit_bytes=56 * 1024 * 1024
+        ),
+    )(
+        query_latent,
+        kv_cache,
+        mask,
+        local_map,
+        jnp.swapaxes(uq_stored, 1, 2),
+        jnp.swapaxes(uk_stored, 1, 2),
+        jnp.swapaxes(uv_stored, 1, 2),
+        out_stored,
+    )
+
+
+def choose_local(mesh):
+    n_row, n_head, n_sub = mesh.shape["row"], mesh.shape["head"], mesh.shape["sub"]
+
+    def local(query_latent, kv_cache, row_lengths, head_map, uq, uk, uv, out_stored):
+        args = (query_latent, kv_cache, row_lengths, head_map, uq, uk, uv, out_stored)
+        n = n_row * n_head
+        batch = query_latent.shape[0] * n_row
+        fits = (
+            mesh.shape["group"] == 2
+            and n_sub == 2
+            and n_head >= 2
+            and n >= 4
+            and out_stored.shape[1] % 16 == 0
+            and out_stored.shape[2] % 512 == 0
+            and uq.shape[0] % (8 * n) == 0
+            and uq.shape[1] % 128 == 0
+            and uk.shape[1] % 128 == 0
+            and uq.shape[2] % 16 == 0
+            and 2 * uq.shape[2] % 128 == 0
+            and batch % (16 * n) == 0
+            and batch % (16 * n_head * n_sub) == 0
+        )
+        if fits:
+            return local_fast(n_row, n_head, n_sub, *args)
+        return local_general(*args)
+
+    return local
+
+
 def solution(mesh):
     in_specs = (
         P(("group", "row"), None),
@@ -101,4 +559,5 @@
         P("sub", "head", "row"),
     )
     out_specs = P(("group", "head", "sub"), "row")
+    local = choose_local(mesh)
     return jax.shard_map(local, mesh=mesh, in_specs=in_specs, out_specs=out_specs, check_vma=False)

time: 742 us -> 134 us (0.18)
  waiting for transfers between devices: 551 us -> 0 us
  Pallas kernels: 0 us -> 128 us
  matrix products: 64.5 us -> 0 us
  local copies, waits for them, and re-layouts: 41.9 us -> 2.28 us
  blocking collectives: 29.5 us -> 0 us
  starting transfers between devices: 20.9 us -> 0 us
  between operations: 13.6 us -> 0.01 us
  other arithmetic: 11.5 us -> 1.99 us
    all_gather x5 -> x0, waiting for transfers between devices: 428 us -> none  [the longest x1 359 us: local(): piece = lax.all_gather(kv_cache, 'head', axis=0, tiled=True)]
    pallas_call x0 -> x1, Pallas kernels: none -> 128 us  [local_fast(): pl.pallas_call(functools.partial(attention_kernel, n_row, n_head, 1.0 / m...]
    all_to_all x3 -> x0, waiting for transfers between devices: 93.5 us -> none  [the longest x1 60.8 us: local(): lax.all_to_all(query_up, 'head', split_axis=0, concat_axis=1, tiled=True)]
    dot_general x6 -> x0, matrix products: 64.5 us -> none  [the longest x1 39.2 us: local(): jnp.einsum('rhk,hko->ro', gathered, absorbed_o, preferred_element_type=jn...]
    all_to_all x7 -> x0, local copies, waits for them, and re-layouts: 31.4 us -> none  [the longest x1 13.6 us: local(): lax.all_to_all(out_stored, 'head', split_axis=0, concat_axis=1, tiled=True)]
    all_to_all x1 -> x0, blocking collectives: 29.5 us -> none  [local(): lax.all_to_all(value_up, 'head', split_axis=0, concat_axis=1, tiled=True)]
    reduce_scatter x1 -> x0, waiting for transfers between devices: 29.4 us -> none  [local(): lax.psum_scatter(jnp.einsum('rhk,hko->ro', gathered, absorbed_o, preferre...]
    all_to_all x3 -> x0, starting transfers between devices: 20.3 us -> none  [the longest x1 8.35 us: local(): lax.all_to_all(out_stored, 'head', split_axis=0, concat_axis=1, tiled=True)]
  transfers between devices with their start and end apart: 9 -> 0, of which waited for: 7 -> 0; matrix products, arithmetic and copies ran while one was open for 7% -> 0% of each run, Pallas kernels for 0% -> 0%
where the time goes in v2:
time: 134 us; the launch traced here: 132 us
  Pallas kernels  128 us (96%)
  local copies, waits for them, and re-layouts  2.28 us (2%)
  other arithmetic  1.99 us (1%)
    pallas_call x1, Pallas kernels, local_fast(): pl.pallas_call(functools.partial(attention_kernel, n_row, n_head, 1.0 / m...  128 us

profile of v2, /device:TPU:13, one launch (start us, length us, event | category | flops | bytes accessed | tf_op | source)
XLA Modules:
  0.0 132.0 jit_solution(3049945206628307402)
XLA Ops:
  0.0 1.3 dynamic-slice_subtract_fusion.map_ref
  1.3 0.7 dynamic_slice.6
  2.0 0.7 fusion.mask_ref
  2.7 127.7 %shard_map.82 = bf16[16,3584]{1,0:T(8,128)(2,1)} custom-call(bf16[64,1536]{1,0:T(8,128)(2,1)} %ql_ref.1, bf16[16,128,512]{2,1,0:T(8,128)(2,1)} %kv_ref.1, s32[16,128]{1,0:T(8,128)} %fusion.mask_ref, s32[64]{0:T(128)} %dynamic-slice_subtract_fusion.map_ref, bf16[64,64,384]{2,1,0:T(8,128)(2,1)} %bitcast.3, bf16[64,64,128]{2,1,0:T(8,128)(2,1)} %bitcast.4, ...), custom_call_target="tpu_custom_call" | custom-call | tf_op jit(solution)/shard_map/pallas_call | solution.py:474
  130.5 1.6 %copy.10 = bf16[16,3584]{1,0:T(8,128)(2,1)} copy(bf16[16,3584]{1,0:T(8,128)(2,1)} %shard_map.82) | data formatting | bytes 229376

commit v3 on v2

--- a/solution.py
+++ b/solution.py
@@ -102,14 +102,16 @@
     n_head,
     scale,
     ql_ref,
-    kv_ref,
+    kv_hbm,
     mask_ref,
     map_ref,
-    uq_ref,
+    uq_hbm,
     uk_ref,
     uv_ref,
     out_hbm,
     result,
+    uq_ref,
+    kv_ref,
     lat,
     q_send,
     q_recv,
@@ -194,6 +196,12 @@
             block = dst.at[peer, other]
             remote(phase + 1, k, block, block, peer, {"group": 1 - group}).wait_recv()
 
+    uq_load = pltpu.make_async_copy(uq_hbm, uq_ref, load_sem.at[1])
+    kv_load = pltpu.make_async_copy(kv_hbm, kv_ref, load_sem.at[2])
+    mine = pl.ds(me * per, per)
+    uk_load = pltpu.make_async_copy(uk_ref.at[mine], uk_recv.at[me], load_sem.at[3])
+    uv_load = pltpu.make_async_copy(uv_ref.at[mine], uv_recv.at[me], load_sem.at[4])
+    uq_load.start()
     barrier = pltpu.get_barrier_semaphore()
     for peer in peers:
         pl.semaphore_signal(barrier, inc=1, device_id=place(peer), device_id_type=MESH)
@@ -206,15 +214,12 @@
     for k, other in enumerate(others):
         send(0, k, ql_ref.at[:, columns], lat.at[row], other * n_head + head)
     send_weights(2, uk_ref, uk_recv)
-    load = pltpu.make_async_copy(out_hbm, out_up, load_sem)
-    load.start()
+    load = pltpu.make_async_copy(out_hbm, out_up, load_sem.at[0])
     lat[row] = ql_ref[:, columns]
-    mine = pl.ds(me * per, per)
-    uk_recv[me] = uk_ref[mine]
-    uv_recv[me] = uv_ref[mine]
     for k, other in enumerate(others):
         arrived(0, k, lat.at[other], other * n_head + head)
     latent = lat[...].reshape(batch, part)
+    uq_load.wait()
 
     for k, peer in enumerate(peers + [me]):
         for at in range(pairs):
@@ -229,6 +234,10 @@
         if k < n - 1:
             send(1, k, q_send.at[peer], q_recv.at[me], peer)
     send_weights(8, uv_ref, uv_recv)
+    uk_load.start()
+    uv_load.start()
+    kv_load.start()
+    load.start()
     pass_weights(2, uk_recv)
 
     share = out_hbm.shape[1]
@@ -258,6 +267,9 @@
                 jnp.concatenate([s[:, which * half : (which + 1) * half] for s in sums], axis=1)
             )
     await_weights(2, uk_recv)
+    uk_load.wait()
+    uv_load.wait()
+    kv_load.wait()
 
     def joined(ref, slot):
         return jnp.concatenate(
@@ -474,12 +486,17 @@
     return pl.pallas_call(
         functools.partial(attention_kernel, n_row, n_head, 1.0 / math.sqrt(DH)),
         out_shape=jax.ShapeDtypeStruct((batch // (n_head * n_sub), wide_out), BF16),
-        in_specs=[vmem] * 3
-        + [pl.BlockSpec(memory_space=pltpu.SMEM)]
-        + [vmem] * 3
-        + [pl.BlockSpec(memory_space=pl.ANY)],
+        in_specs=[
+            vmem,
+            pl.BlockSpec(memory_space=pl.ANY),
+            vmem,
+            pl.BlockSpec(memory_space=pltpu.SMEM),
+        ]
+        + [pl.BlockSpec(memory_space=pl.ANY)] * 4,
         out_specs=vmem,
         scratch_shapes=[
+            pltpu.VMEM((slots, half, part), BF16),
+            pltpu.VMEM(kv_cache.shape, BF16),
             pltpu.VMEM((n_row, rows, part), BF16),
             pltpu.VMEM((n, per // 2, batch, 2 * half), BF16),
             pltpu.VMEM((n, per // 2, batch, 2 * half), BF16),
@@ -501,10 +518,10 @@
             sums,
             pltpu.SemaphoreType.DMA((13 + chunks, n)),
             pltpu.SemaphoreType.DMA((13 + chunks, n)),
-            pltpu.SemaphoreType.DMA,
+            pltpu.SemaphoreType.DMA((5,)),
         ],
         compiler_params=pltpu.CompilerParams(
-            collective_id=0, has_side_effects=True, vmem_limit_bytes=56 * 1024 * 1024
+            collective_id=0, has_side_effects=True, vmem_limit_bytes=60 * 1024 * 1024
         ),
     )(
         query_latent,

time: 134 us -> 132 us (0.985)
  Pallas kernels: 128 us -> 126 us
    pallas_call x1, Pallas kernels: 128 us -> 126 us  [local_fast(): pl.pallas_call(functools.partial(attention_kernel, n_row, n_head, 1.0 / m...]
where the time goes in v3:
time: 132 us; the launch traced here: 130 us
  Pallas kernels  126 us (95%)
  local copies, waits for them, and re-layouts  2.28 us (2%)
  other arithmetic  1.99 us (2%)
    pallas_call x1, Pallas kernels, local_fast(): pl.pallas_call(functools.partial(attention_kernel, n_row, n_head, 1.0 / m...  126 us

profile of v3, /device:TPU:13, one launch (start us, length us, event | category | flops | bytes accessed | tf_op | source)
XLA Modules:
  0.0 130.0 jit_solution(12607855148515732286)
XLA Ops:
  0.0 1.3 %dynamic-slice_subtract_fusion.map_ref = s32[64]{0:T(128)} fusion(s32[128]{0:T(128)} %param.11, s32[]{:T(128)S(6)} %select_n.7, s32[]{:T(128)S(6)} %mul.7), kind=kLoop, calls=%fused_computation.2 | loop fusion | flops 64 | bytes 520 | tf_op jit(solution)/shard_map/sub | solution.py:480
  1.3 0.7 dynamic_slice.6
  2.0 0.7 fusion.mask_ref
  2.7 125.8 %shard_map.82 = bf16[16,3584]{1,0:T(8,128)(2,1)} custom-call(bf16[64,1536]{1,0:T(8,128)(2,1)} %ql_ref.1, bf16[16,128,512]{2,1,0:T(8,128)(2,1)} %kv_hbm.1, s32[16,128]{1,0:T(8,128)} %fusion.mask_ref, s32[64]{0:T(128)} %dynamic-slice_subtract_fusion.map_ref, bf16[64,64,384]{2,1,0:T(8,128)(2,1)} %bitcast.3, bf16[64,64,128]{2,1,0:T(8,128)(2,1)} %bitcast.4, ...), custom_call_target="tpu_custom_call" | custom-call | tf_op jit(solution)/shard_map/pallas_call | solution.py:486
  128.5 1.6 %copy.10 = bf16[16,3584]{1,0:T(8,128)(2,1)} copy(bf16[16,3584]{1,0:T(8,128)(2,1)} %shard_map.82) | data formatting | bytes 229376
